TPU v7x, 512 devices: a whole 4x8x8 slice. The times are simulated.
512 devices in a mesh: outer: 16 (over x, y_lo, core), inner: 32 (over y_hi, z).
Axes of the slice: x: 4, y: 8 (y_hi: 4, y_lo: 2; y = y_hi * 2 + y_lo), z: 8, core: 2. Of those that a mesh axis runs over, the one named last changes fastest.
Arguments:
- queries: bfloat16 [65536, 4096], P(('outer', 'inner'))
- keys: bfloat16 [65536, 512], P(('outer', 'inner'))
- values: bfloat16 [65536, 512], P(('outer', 'inner')), may hold values from -6 to 6
- grad_out: bfloat16 [65536, 4096], P(('outer', 'inner')), may hold values from -6 to 6
- doc_start: int32 [65536], P(('outer', 'inner')), may hold values from 0 to 65535, as said below
Outputs:
- grad_queries: bfloat16 [65536, 4096], P(('outer', 'inner'))
- grad_keys: bfloat16 [65536, 512], P(('outer', 'inner'))
- grad_values: bfloat16 [65536, 512], P(('outer', 'inner'))
Inputs may be any that keep to these rules, and one draw needn't show every extreme that they name: doc_start is non-decreasing along the sequence and doc_start[t] <= t; equal values mark one document; every document has 1 to 512 tokens and the first has exactly 512.
All inputs are finite; a program needn't handle non-finite values.
Results may differ from a plain program's by a relative error of at most 0.012.
The roundings to bfloat16 on the way count: a program that leaves them out, or rounds other values in their place, can miss the bound.
Values may be sent and summed in bfloat16 or wider, within the bound.
No kernel may reach another device: no remote copies, remote signals or barrier semaphores. Data moves between devices by JAX's collectives and lax.ppermute only.
A program may use at most 128 MiB of HBM per device.

v0:
```python
import jax
import jax.numpy as jnp
from jax import lax
from jax.sharding import PartitionSpec as P

HEAD_SIZE = 128
SPAN = 4


def passed_along(shard, axis, by):
    peers = lax.axis_size(axis)
    pairs = [(i, i + by) for i in range(peers) if 0 <= i + by < peers]
    return lax.ppermute(shard, axis, pairs)


def head_group(
    queries, grad_out, key_window, value_window, visible_mask, group, query_per_key_head, head_dim
):
    tok_rows = queries.shape[0]
    width = key_window.shape[0]
    factor = head_dim ** (-0.5)
    q_part = queries.reshape(tok_rows, -1, query_per_key_head * head_dim)[:, group].reshape(
        tok_rows * query_per_key_head, head_dim
    )
    g_part = grad_out.reshape(tok_rows, -1, query_per_key_head * head_dim)[:, group].reshape(
        tok_rows * query_per_key_head, head_dim
    )
    k_part = key_window.reshape(width, -1, head_dim)[:, group]
    v_part = value_window.reshape(width, -1, head_dim)[:, group]
    scores = jnp.dot(q_part, k_part.T, preferred_element_type=jnp.float32) * factor
    mask_rows = jnp.broadcast_to(
        visible_mask[:, None, :], (tok_rows, query_per_key_head, width)
    ).reshape(tok_rows * query_per_key_head, width)
    top_score = jnp.max(jnp.where(mask_rows, scores, -1e30), axis=1, keepdims=True)
    expo = jnp.where(mask_rows, jnp.exp(scores - top_score), 0.0)
    probs = expo / jnp.sum(expo, axis=1, keepdims=True)
    probs_low = probs.astype(jnp.bfloat16)
    attn_out = jnp.dot(probs_low, v_part, preferred_element_type=jnp.float32)
    delta = jnp.sum(g_part.astype(jnp.float32) * attn_out, axis=1, keepdims=True)
    dprobs = jnp.dot(g_part, v_part.T, preferred_element_type=jnp.float32)
    dscores = (probs * (dprobs - delta)).astype(jnp.bfloat16)
    query_gradient = jnp.dot(dscores, k_part, preferred_element_type=jnp.float32) * factor
    key_gradient = jnp.dot(dscores.T, q_part, preferred_element_type=jnp.float32) * factor
    value_gradient = jnp.dot(probs_low.T, g_part, preferred_element_type=jnp.float32)
    return (
        query_gradient.reshape(tok_rows, query_per_key_head * head_dim),
        key_gradient,
        value_gradient,
    )


def block_gradient_step(
    queries,
    grad_out,
    key_window,
    value_window,
    visible_mask,
    heads_kv,
    query_per_key_head,
    head_dim,
):
    dq_list, dk_list, dv_list = ([], [], [])
    for group in range(heads_kv):
        query_gradient, key_gradient, value_gradient = head_group(
            queries,
            grad_out,
            key_window,
            value_window,
            visible_mask,
            group,
            query_per_key_head,
            head_dim,
        )
        dq_list.append(query_gradient)
        dk_list.append(key_gradient)
        dv_list.append(value_gradient)
    return (
        jnp.concatenate(dq_list, axis=1),
        jnp.concatenate(dk_list, axis=1),
        jnp.concatenate(dv_list, axis=1),
    )


def body(queries, keys, values, grad_out, doc_start):
    tok_rows = queries.shape[0]
    kv_cols = keys.shape[1]
    heads_kv = kv_cols // HEAD_SIZE
    query_per_key_head = queries.shape[1] // kv_cols
    width = (SPAN + 1) * tok_rows
    key_list = [keys]
    val_list = [values]
    moving = (keys, values)
    for offset in range(SPAN):
        moving = passed_along((moving[0], moving[1]), ("outer", "inner"), 1)
        key_list.insert(0, moving[0])
        val_list.insert(0, moving[1])
    key_window = jnp.concatenate(key_list, axis=0)
    value_window = jnp.concatenate(val_list, axis=0)
    base_pos = lax.axis_index(("outer", "inner")) * tok_rows
    q_pos = base_pos + jnp.arange(tok_rows, dtype=jnp.int32)
    k_pos = base_pos - SPAN * tok_rows + jnp.arange(width, dtype=jnp.int32)
    visible_mask = (k_pos[None, :] >= doc_start[:, None]) & (k_pos[None, :] <= q_pos[:, None])
    query_gradient, key_gradient, value_gradient = block_gradient_step(
        queries,
        grad_out,
        key_window,
        value_window,
        visible_mask,
        heads_kv,
        query_per_key_head,
        HEAD_SIZE,
    )
    low_k = lax.optimization_barrier(key_gradient.astype(jnp.bfloat16))
    low_v = lax.optimization_barrier(value_gradient.astype(jnp.bfloat16))

    def owner_term(offset):
        first_row = (SPAN - offset) * tok_rows
        return (low_k[first_row : first_row + tok_rows], low_v[first_row : first_row + tok_rows])

    start_k, start_v = owner_term(SPAN)
    total_k = start_k.astype(jnp.float32)
    total_v = start_v.astype(jnp.float32)
    for offset in range(SPAN - 1, -1, -1):
        total_k, total_v = passed_along((total_k, total_v), ("outer", "inner"), -1)
        extra_k, extra_v = owner_term(offset)
        total_k = total_k + extra_k.astype(jnp.float32)
        total_v = total_v + extra_v.astype(jnp.float32)
    return (
        query_gradient.astype(jnp.bfloat16),
        total_k.astype(jnp.bfloat16),
        total_v.astype(jnp.bfloat16),
    )


def solution(mesh):
    in_specs = (
        P(("outer", "inner"), None),
        P(("outer", "inner"), None),
        P(("outer", "inner"), None),
        P(("outer", "inner"), None),
        P(("outer", "inner")),
    )
    out_specs = (
        P(("outer", "inner"), None),
        P(("outer", "inner"), None),
        P(("outer", "inner"), None),
    )
    return jax.shard_map(body, mesh=mesh, in_specs=in_specs, out_specs=out_specs, check_vma=False)
```

profile of v0, /device:TPU:7, one launch (start us, length us, event | category | flops | bytes accessed | tf_op | source)
XLA Modules:
  0.0 180.8 jit_solution(6884426052923758347)
XLA Ops:
  0.6 1.0 copy.32
  1.7 4.0 %collective-permute-start = (bf16[128,512]{0,1:T(8,128)(2,1)S(1)}, bf16[128,512]{0,1:T(8,128)(2,1)}, u32[]{:S(2)}, u32[]{:S(2)}) collective-permute-start(bf16[128,512]{0,1:T(8,128)(2,1)S(1)} %copy.32), channel_id=1, source_target_pairs={{0,1},{1,2},{2,3},{3,4},{4,5},{5,6},{6,7},{7,8},{8,9},{9,10},{10,1... | collective-permute-start | bytes 393224 | tf_op jit(solution)/shard_map/ppermute | solution.py:13
  5.7 1.0 copy.38
  6.7 4.0 %collective-permute-start.4 = (bf16[128,512]{0,1:T(8,128)(2,1)S(1)}, bf16[128,512]{0,1:T(8,128)(2,1)S(1)}, u32[]{:S(2)}, u32[]{:S(2)}) collective-permute-start(bf16[128,512]{0,1:T(8,128)(2,1)S(1)} %copy.38), channel_id=1, source_target_pairs={{0,1},{1,2},{2,3},{3,4},{4,5},{5,6},{6,7},{7,8},{8,9},{9,10},{10,1... | collective-permute-start | bytes 393224 | tf_op jit(solution)/shard_map/ppermute | solution.py:13
  10.7 1.9 %reshape.121 = bf16[128,4,1024]{2,1,0:T(4,128)(2,1)S(1)} reshape(bf16[128,4096]{1,0:T(8,128)(2,1)} %param.5) | data formatting | bytes 2097152 | tf_op jit(solution)/shard_map/reshape | solution.py:22
  12.6 5.3 %slice_reduce_fusion.7 = (bf16[128,1024]{1,0:T(8,128)(2,1)S(1)}, bf16[128,1024]{1,0:T(8,128)(2,1)S(1)}, bf16[128,1024]{1,0:T(8,128)(2,1)S(1)}, bf16[128,1024]{1,0:T(8,128)(2,1)S(1)}) fusion(bf16[128,4,1024]{2,1,0:T(4,128)(2,1)S(1)} %reshape.121), kind=kLoop, calls=%fused_computation.83 | loop fusion | bytes 2097152 | tf_op jit(solution)/shard_map/slice | solution.py:22
  17.9 1.9 %reshape.123 = bf16[128,4,1024]{2,1,0:T(4,128)(2,1)S(1)} reshape(bf16[128,4096]{1,0:T(8,128)(2,1)} %param.8) | data formatting | bytes 2097152 | tf_op jit(solution)/shard_map/reshape | solution.py:25
  19.8 5.3 %slice_reduce_fusion.6 = (bf16[128,1024]{1,0:T(8,128)(2,1)S(1)}, bf16[128,1024]{1,0:T(8,128)(2,1)S(1)}, bf16[128,1024]{1,0:T(8,128)(2,1)S(1)}, bf16[128,1024]{1,0:T(8,128)(2,1)S(1)}) fusion(bf16[128,4,1024]{2,1,0:T(4,128)(2,1)S(1)} %reshape.123), kind=kLoop, calls=%fused_computation.82 | loop fusion | bytes 2097152 | tf_op jit(solution)/shard_map/slice | solution.py:25
  25.1 4.0 %collective-permute-start.1 = (bf16[128,512]{0,1:T(8,128)(2,1)}, bf16[128,512]{0,1:T(8,128)(2,1)}, u32[]{:S(2)}, u32[]{:S(2)}) collective-permute-start(bf16[128,512]{0,1:T(8,128)(2,1)} %collective-permute-done), channel_id=1, source_target_pairs={{0,1},{1,2},{2,3},{3,4},{4,5},{5,6},{6,7},{7,8},{8,9},{9,10},{10,1... | collective-permute-start | bytes 393224 | tf_op jit(solution)/shard_map/ppermute | solution.py:13
  29.2 5.2 %collective-permute-start.5 = (bf16[128,512]{0,1:T(8,128)(2,1)S(1)}, bf16[128,512]{0,1:T(8,128)(2,1)}, u32[]{:S(2)}, u32[]{:S(2)}) collective-permute-start(bf16[128,512]{0,1:T(8,128)(2,1)S(1)} %collective-permute-done.4), channel_id=1, source_target_pairs={{0,1},{1,2},{2,3},{3,4},{4,5},{5,6},{6,7},{7,8},{8,9},{9,10},{10,1... | collective-permute-start | bytes 393224 | tf_op jit(solution)/shard_map/ppermute | solution.py:13
  34.4 11.4 %collective-permute-done.1 = bf16[128,512]{0,1:T(8,128)(2,1)} collective-permute-done((bf16[128,512]{0,1:T(8,128)(2,1)}, bf16[128,512]{0,1:T(8,128)(2,1)}, u32[]{:S(2)}, u32[]{:S(2)}) %collective-permute-start.1) | collective-permute-done | bytes 131104 | tf_op jit(solution)/shard_map/ppermute | solution.py:13
  45.8 1.9 %collective-permute-start.2 = (bf16[128,512]{0,1:T(8,128)(2,1)}, bf16[128,512]{0,1:T(8,128)(2,1)}, u32[]{:S(2)}, u32[]{:S(2)}) collective-permute-start(bf16[128,512]{0,1:T(8,128)(2,1)} %collective-permute-done.1), channel_id=1, source_target_pairs={{0,1},{1,2},{2,3},{3,4},{4,5},{5,6},{6,7},{7,8},{8,9},{9,10},{10,1... | collective-permute-start | bytes 393224 | tf_op jit(solution)/shard_map/ppermute | solution.py:13
  47.9 1.9 %collective-permute-start.6 = (bf16[128,512]{0,1:T(8,128)(2,1)}, bf16[128,512]{0,1:T(8,128)(2,1)}, u32[]{:S(2)}, u32[]{:S(2)}) collective-permute-start(bf16[128,512]{0,1:T(8,128)(2,1)} %collective-permute-done.5), channel_id=1, source_target_pairs={{0,1},{1,2},{2,3},{3,4},{4,5},{5,6},{6,7},{7,8},{8,9},{9,10},{10,1... | collective-permute-start | bytes 393224 | tf_op jit(solution)/shard_map/ppermute | solution.py:13
  49.8 8.4 %collective-permute-done.2 = bf16[128,512]{0,1:T(8,128)(2,1)} collective-permute-done((bf16[128,512]{0,1:T(8,128)(2,1)}, bf16[128,512]{0,1:T(8,128)(2,1)}, u32[]{:S(2)}, u32[]{:S(2)}) %collective-permute-start.2) | collective-permute-done | bytes 131104 | tf_op jit(solution)/shard_map/ppermute | solution.py:13
  58.3 1.9 %collective-permute-start.3 = (bf16[128,512]{0,1:T(8,128)(2,1)}, bf16[128,512]{0,1:T(8,128)(2,1)}, u32[]{:S(2)}, u32[]{:S(2)}) collective-permute-start(bf16[128,512]{0,1:T(8,128)(2,1)} %collective-permute-done.2), channel_id=1, source_target_pairs={{0,1},{1,2},{2,3},{3,4},{4,5},{5,6},{6,7},{7,8},{8,9},{9,10},{10,1... | collective-permute-start | bytes 393224 | tf_op jit(solution)/shard_map/ppermute | solution.py:13
  65.0 2.1 %collective-permute-start.7 = (bf16[128,512]{0,1:T(8,128)(2,1)}, bf16[128,512]{0,1:T(8,128)(2,1)S(1)}, u32[]{:S(2)}, u32[]{:S(2)}) collective-permute-start(bf16[128,512]{0,1:T(8,128)(2,1)} %collective-permute-done.6), channel_id=1, source_target_pairs={{0,1},{1,2},{2,3},{3,4},{4,5},{5,6},{6,7},{7,8},{8,9},{9,10},{10,1... | collective-permute-start | bytes 393224 | tf_op jit(solution)/shard_map/ppermute | solution.py:13
  67.1 3.2 %collective-permute-done.3 = bf16[128,512]{0,1:T(8,128)(2,1)} collective-permute-done((bf16[128,512]{0,1:T(8,128)(2,1)}, bf16[128,512]{0,1:T(8,128)(2,1)}, u32[]{:S(2)}, u32[]{:S(2)}) %collective-permute-start.3) | collective-permute-done | bytes 131104 | tf_op jit(solution)/shard_map/ppermute | solution.py:13
  71.2 0.9 constant_dynamic-update-slice_fusion.3
  75.8 2.0 %fusion.17 = (f32[1024]{0:T(1024)S(1)}, f32[1024]{0:T(1024)S(1)}, f32[1024]{0:T(1024)S(1)}, f32[1024]{0:T(1024)S(1)}, f32[640,1024]{1,0:T(8,128)S(1)}) fusion(pred[1024,640]{0,1:T(32,128)(4,1)S(1)} %copy.37, f32[640,1024]{1,0:T(8,128)S(1)} %get-tuple-element.28, f32[1024]{0:T(1024)S(1)} %get-tuple-element.27, f32[640,1024]{1,0:T(8,128)S(1)} %fusion.46, ...), kind=kOutput, calls=%fused_computation.29 | convolution fusion | flops 176287744 | bytes 11587584 | tf_op jit(solution)/shard_map/dot_general | solution.py:30
  77.8 1.0 convolution_convert_fusion.3
  80.8 1.0 fusion.28
  81.8 1.0 fusion.12
  84.0 1.7 fusion.19
  85.7 0.9 convolution_convert_fusion.2
  86.6 0.9 convolution_convert_fusion.1
  88.9 4.7 %collective-permute-start.12 = (f32[128,512]{0,1:T(8,128)S(1)}, f32[128,512]{0,1:T(8,128)S(1)}, u32[]{:S(2)}, u32[]{:S(2)}) collective-permute-start(f32[128,512]{0,1:T(8,128)S(1)} %slice_convert_fusion), channel_id=1, source_target_pairs={{1,0},{2,1},{3,2},{4,3},{5,4},{6,5},{7,6},{8,7},{9,8},{10,9},{11,1... | collective-permute-start | bytes 786440 | tf_op jit(solution)/shard_map/ppermute | solution.py:13
  93.6 1.0 fusion.29
  94.6 1.0 fusion.8
  96.2 1.0 fusion.30
  97.2 1.0 fusion.4
  98.9 1.0 fusion.31
  99.9 1.0 fusion
  101.6 3.9 %collective-permute-start.8 = (f32[128,512]{0,1:T(8,128)S(1)}, f32[128,512]{0,1:T(8,128)S(1)}, u32[]{:S(2)}, u32[]{:S(2)}) collective-permute-start(f32[128,512]{0,1:T(8,128)S(1)} %slice_convert_fusion.1), channel_id=1, source_target_pairs={{1,0},{2,1},{3,2},{4,3},{5,4},{6,5},{7,6},{8,7},{9,8},{10,9},{11,1... | collective-permute-start | bytes 786440 | tf_op jit(solution)/shard_map/ppermute | solution.py:13
  106.2 1.9 %collective-permute-start.13 = (f32[128,512]{0,1:T(8,128)S(1)}, f32[128,512]{0,1:T(8,128)S(1)}, u32[]{:S(2)}, u32[]{:S(2)}) collective-permute-start(f32[128,512]{0,1:T(8,128)S(1)} %convert_add_fusion.2), channel_id=1, source_target_pairs={{1,0},{2,1},{3,2},{4,3},{5,4},{6,5},{7,6},{8,7},{9,8},{10,9},{11,1... | collective-permute-start | bytes 786440 | tf_op jit(solution)/shard_map/ppermute | solution.py:13
  108.1 11.2 %collective-permute-done.8 = f32[128,512]{0,1:T(8,128)S(1)} collective-permute-done((f32[128,512]{0,1:T(8,128)S(1)}, f32[128,512]{0,1:T(8,128)S(1)}, u32[]{:S(2)}, u32[]{:S(2)}) %collective-permute-start.8) | collective-permute-done | bytes 262176 | tf_op jit(solution)/shard_map/ppermute | solution.py:13
  119.3 9.1 %collective-permute-start.9 = (f32[128,512]{0,1:T(8,128)S(1)}, f32[128,512]{0,1:T(8,128)S(1)}, u32[]{:S(2)}, u32[]{:S(2)}) collective-permute-start(f32[128,512]{0,1:T(8,128)S(1)} %convert_add_fusion.5), channel_id=1, source_target_pairs={{1,0},{2,1},{3,2},{4,3},{5,4},{6,5},{7,6},{8,7},{9,8},{10,9},{11,1... | collective-permute-start | bytes 786440 | tf_op jit(solution)/shard_map/ppermute | solution.py:13
  129.0 1.7 collective-permute-done.13
  130.7 9.1 %collective-permute-start.14 = (f32[128,512]{0,1:T(8,128)S(1)}, f32[128,512]{0,1:T(8,128)S(1)}, u32[]{:S(2)}, u32[]{:S(2)}) collective-permute-start(f32[128,512]{0,1:T(8,128)S(1)} %convert_add_fusion.1), channel_id=1, source_target_pairs={{1,0},{2,1},{3,2},{4,3},{5,4},{6,5},{7,6},{8,7},{9,8},{10,9},{11,1... | collective-permute-start | bytes 786440 | tf_op jit(solution)/shard_map/ppermute | solution.py:13
  139.9 2.1 %collective-permute-done.9 = f32[128,512]{0,1:T(8,128)S(1)} collective-permute-done((f32[128,512]{0,1:T(8,128)S(1)}, f32[128,512]{0,1:T(8,128)S(1)}, u32[]{:S(2)}, u32[]{:S(2)}) %collective-permute-start.9) | collective-permute-done | bytes 262176 | tf_op jit(solution)/shard_map/ppermute | solution.py:13
  142.0 9.1 %collective-permute-start.10 = (f32[128,512]{0,1:T(8,128)S(1)}, f32[128,512]{0,1:T(8,128)}, u32[]{:S(2)}, u32[]{:S(2)}) collective-permute-start(f32[128,512]{0,1:T(8,128)S(1)} %convert_add_fusion.4), channel_id=1, source_target_pairs={{1,0},{2,1},{3,2},{4,3},{5,4},{6,5},{7,6},{8,7},{9,8},{10,9},{11,1... | collective-permute-start | bytes 786440 | tf_op jit(solution)/shard_map/ppermute | solution.py:13
  151.1 1.3 fusion.27
  152.7 1.1 reshape.127
  153.8 8.5 %collective-permute-start.15 = (f32[128,512]{0,1:T(8,128)S(1)}, f32[128,512]{0,1:T(8,128)S(1)}, u32[]{:S(2)}, u32[]{:S(2)}) collective-permute-start(f32[128,512]{0,1:T(8,128)S(1)} %convert_add_fusion), channel_id=1, source_target_pairs={{1,0},{2,1},{3,2},{4,3},{5,4},{6,5},{7,6},{8,7},{9,8},{10,9},{11,1... | collective-permute-start | bytes 786440 | tf_op jit(solution)/shard_map/ppermute | solution.py:13
  162.3 2.1 %collective-permute-done.10 = f32[128,512]{0,1:T(8,128)} collective-permute-done((f32[128,512]{0,1:T(8,128)S(1)}, f32[128,512]{0,1:T(8,128)}, u32[]{:S(2)}, u32[]{:S(2)}) %collective-permute-start.10) | collective-permute-done | bytes 262176 | tf_op jit(solution)/shard_map/ppermute | solution.py:13
  164.4 1.0 convert_add_fusion.3
  165.4 9.2 %collective-permute-start.11 = (f32[128,512]{0,1:T(8,128)S(1)}, f32[128,512]{0,1:T(8,128)S(1)}, u32[]{:S(2)}, u32[]{:S(2)}) collective-permute-start(f32[128,512]{0,1:T(8,128)S(1)} %convert_add_fusion.3), channel_id=1, source_target_pairs={{1,0},{2,1},{3,2},{4,3},{5,4},{6,5},{7,6},{8,7},{9,8},{10,9},{11,1... | collective-permute-start | bytes 786440 | tf_op jit(solution)/shard_map/ppermute | solution.py:13
  174.6 1.0 pad_maximum_fusion
  176.5 3.6 %collective-permute-done.11 = f32[128,512]{0,1:T(8,128)S(1)} collective-permute-done((f32[128,512]{0,1:T(8,128)S(1)}, f32[128,512]{0,1:T(8,128)S(1)}, u32[]{:S(2)}, u32[]{:S(2)}) %collective-permute-start.11) | collective-permute-done | bytes 262176 | tf_op jit(solution)/shard_map/ppermute | solution.py:13
  (77 shorter events, 18.8 us)
Async XLA Ops:
  1.7 16.2 %copy-start = (bf16[128,512]{0,1:T(8,128)(2,1)}, bf16[128,512]{0,1:T(8,128)(2,1)S(1)}, u32[]{:S(2)}) copy-start(bf16[128,512]{0,1:T(8,128)(2,1)S(1)} %copy.32) | copy-start | bytes 393220
  1.7 23.5 %collective-permute-start = (bf16[128,512]{0,1:T(8,128)(2,1)S(1)}, bf16[128,512]{0,1:T(8,128)(2,1)}, u32[]{:S(2)}, u32[]{:S(2)}) collective-permute-start(bf16[128,512]{0,1:T(8,128)(2,1)S(1)} %copy.32), channel_id=1, source_target_pairs={{0,1},{1,2},{2,3},{3,4},{4,5},{5,6},{6,7},{7,8},{8,9},{9,10},{10,1... | collective-permute-start | bytes 393224 | tf_op jit(solution)/shard_map/ppermute | solution.py:13
  6.7 22.5 %collective-permute-start.4 = (bf16[128,512]{0,1:T(8,128)(2,1)S(1)}, bf16[128,512]{0,1:T(8,128)(2,1)S(1)}, u32[]{:S(2)}, u32[]{:S(2)}) collective-permute-start(bf16[128,512]{0,1:T(8,128)(2,1)S(1)} %copy.38), channel_id=1, source_target_pairs={{0,1},{1,2},{2,3},{3,4},{4,5},{5,6},{6,7},{7,8},{8,9},{9,10},{10,1... | collective-permute-start | bytes 393224 | tf_op jit(solution)/shard_map/ppermute | solution.py:13
  17.9 29.8 %copy-start.7 = (s32[128]{0:T(128)S(1)}, s32[128]{0:T(128)}, u32[]{:S(2)}) copy-start(s32[128]{0:T(128)} %param.9) | copy-start | bytes 1540
  25.1 20.7 %collective-permute-start.1 = (bf16[128,512]{0,1:T(8,128)(2,1)}, bf16[128,512]{0,1:T(8,128)(2,1)}, u32[]{:S(2)}, u32[]{:S(2)}) collective-permute-start(bf16[128,512]{0,1:T(8,128)(2,1)} %collective-permute-done), channel_id=1, source_target_pairs={{0,1},{1,2},{2,3},{3,4},{4,5},{5,6},{6,7},{7,8},{8,9},{9,10},{10,1... | collective-permute-start | bytes 393224 | tf_op jit(solution)/shard_map/ppermute | solution.py:13
  29.2 32.6 %copy-start.5 = (bf16[128,512]{0,1:T(8,128)(2,1)}, bf16[128,512]{0,1:T(8,128)(2,1)S(1)}, u32[]{:S(2)}) copy-start(bf16[128,512]{0,1:T(8,128)(2,1)S(1)} %collective-permute-done.4) | copy-start | bytes 393220
  29.2 18.7 %collective-permute-start.5 = (bf16[128,512]{0,1:T(8,128)(2,1)S(1)}, bf16[128,512]{0,1:T(8,128)(2,1)}, u32[]{:S(2)}, u32[]{:S(2)}) collective-permute-start(bf16[128,512]{0,1:T(8,128)(2,1)S(1)} %collective-permute-done.4), channel_id=1, source_target_pairs={{0,1},{1,2},{2,3},{3,4},{4,5},{5,6},{6,7},{7,8},{8,9},{9,10},{10,1... | collective-permute-start | bytes 393224 | tf_op jit(solution)/shard_map/ppermute | solution.py:13
  45.8 12.4 %collective-permute-start.2 = (bf16[128,512]{0,1:T(8,128)(2,1)}, bf16[128,512]{0,1:T(8,128)(2,1)}, u32[]{:S(2)}, u32[]{:S(2)}) collective-permute-start(bf16[128,512]{0,1:T(8,128)(2,1)} %collective-permute-done.1), channel_id=1, source_target_pairs={{0,1},{1,2},{2,3},{3,4},{4,5},{5,6},{6,7},{7,8},{8,9},{9,10},{10,1... | collective-permute-start | bytes 393224 | tf_op jit(solution)/shard_map/ppermute | solution.py:13
  47.9 17.0 %collective-permute-start.6 = (bf16[128,512]{0,1:T(8,128)(2,1)}, bf16[128,512]{0,1:T(8,128)(2,1)}, u32[]{:S(2)}, u32[]{:S(2)}) collective-permute-start(bf16[128,512]{0,1:T(8,128)(2,1)} %collective-permute-done.5), channel_id=1, source_target_pairs={{0,1},{1,2},{2,3},{3,4},{4,5},{5,6},{6,7},{7,8},{8,9},{9,10},{10,1... | collective-permute-start | bytes 393224 | tf_op jit(solution)/shard_map/ppermute | solution.py:13
  58.3 12.0 %collective-permute-start.3 = (bf16[128,512]{0,1:T(8,128)(2,1)}, bf16[128,512]{0,1:T(8,128)(2,1)}, u32[]{:S(2)}, u32[]{:S(2)}) collective-permute-start(bf16[128,512]{0,1:T(8,128)(2,1)} %collective-permute-done.2), channel_id=1, source_target_pairs={{0,1},{1,2},{2,3},{3,4},{4,5},{5,6},{6,7},{7,8},{8,9},{9,10},{10,1... | collective-permute-start | bytes 393224 | tf_op jit(solution)/shard_map/ppermute | solution.py:13
  61.8 12.3 %copy-start.1 = (bf16[128,512]{0,1:T(8,128)(2,1)S(1)}, bf16[128,512]{0,1:T(8,128)(2,1)}, u32[]{:S(2)}) copy-start(bf16[128,512]{0,1:T(8,128)(2,1)} %copy-done) | copy-start | bytes 393220
  65.0 13.8 %collective-permute-start.7 = (bf16[128,512]{0,1:T(8,128)(2,1)}, bf16[128,512]{0,1:T(8,128)(2,1)S(1)}, u32[]{:S(2)}, u32[]{:S(2)}) collective-permute-start(bf16[128,512]{0,1:T(8,128)(2,1)} %collective-permute-done.6), channel_id=1, source_target_pairs={{0,1},{1,2},{2,3},{3,4},{4,5},{5,6},{6,7},{7,8},{8,9},{9,10},{10,1... | collective-permute-start | bytes 393224 | tf_op jit(solution)/shard_map/ppermute | solution.py:13
  77.8 2.9 %copy-start.6 = (bf16[128,512]{0,1:T(8,128)(2,1)S(1)}, bf16[128,512]{0,1:T(8,128)(2,1)}, u32[]{:S(2)}) copy-start(bf16[128,512]{0,1:T(8,128)(2,1)} %copy-done.5) | copy-start | bytes 393220
  87.6 6.0 %copy-start.4 = (bf16[1024,128]{0,1:T(8,128)(2,1)S(1)}, bf16[1024,128]{0,1:T(8,128)(2,1)}, u32[]{:S(2)}) copy-start(bf16[1024,128]{0,1:T(8,128)(2,1)} %copy.49) | copy-start | bytes 786436
  88.9 17.3 %collective-permute-start.12 = (f32[128,512]{0,1:T(8,128)S(1)}, f32[128,512]{0,1:T(8,128)S(1)}, u32[]{:S(2)}, u32[]{:S(2)}) collective-permute-start(f32[128,512]{0,1:T(8,128)S(1)} %slice_convert_fusion), channel_id=1, source_target_pairs={{1,0},{2,1},{3,2},{4,3},{5,4},{6,5},{7,6},{8,7},{9,8},{10,9},{11,1... | collective-permute-start | bytes 786440 | tf_op jit(solution)/shard_map/ppermute | solution.py:13
  94.6 1.6 copy-start.3
  97.2 1.6 copy-start.2
  101.6 17.7 %collective-permute-start.8 = (f32[128,512]{0,1:T(8,128)S(1)}, f32[128,512]{0,1:T(8,128)S(1)}, u32[]{:S(2)}, u32[]{:S(2)}) collective-permute-start(f32[128,512]{0,1:T(8,128)S(1)} %slice_convert_fusion.1), channel_id=1, source_target_pairs={{1,0},{2,1},{3,2},{4,3},{5,4},{6,5},{7,6},{8,7},{9,8},{10,9},{11,1... | collective-permute-start | bytes 786440 | tf_op jit(solution)/shard_map/ppermute | solution.py:13
  106.2 24.6 %collective-permute-start.13 = (f32[128,512]{0,1:T(8,128)S(1)}, f32[128,512]{0,1:T(8,128)S(1)}, u32[]{:S(2)}, u32[]{:S(2)}) collective-permute-start(f32[128,512]{0,1:T(8,128)S(1)} %convert_add_fusion.2), channel_id=1, source_target_pairs={{1,0},{2,1},{3,2},{4,3},{5,4},{6,5},{7,6},{8,7},{9,8},{10,9},{11,1... | collective-permute-start | bytes 786440 | tf_op jit(solution)/shard_map/ppermute | solution.py:13
  119.3 22.6 %collective-permute-start.9 = (f32[128,512]{0,1:T(8,128)S(1)}, f32[128,512]{0,1:T(8,128)S(1)}, u32[]{:S(2)}, u32[]{:S(2)}) collective-permute-start(f32[128,512]{0,1:T(8,128)S(1)} %convert_add_fusion.5), channel_id=1, source_target_pairs={{1,0},{2,1},{3,2},{4,3},{5,4},{6,5},{7,6},{8,7},{9,8},{10,9},{11,1... | collective-permute-start | bytes 786440 | tf_op jit(solution)/shard_map/ppermute | solution.py:13
  130.7 23.0 %collective-permute-start.14 = (f32[128,512]{0,1:T(8,128)S(1)}, f32[128,512]{0,1:T(8,128)S(1)}, u32[]{:S(2)}, u32[]{:S(2)}) collective-permute-start(f32[128,512]{0,1:T(8,128)S(1)} %convert_add_fusion.1), channel_id=1, source_target_pairs={{1,0},{2,1},{3,2},{4,3},{5,4},{6,5},{7,6},{8,7},{9,8},{10,9},{11,1... | collective-permute-start | bytes 786440 | tf_op jit(solution)/shard_map/ppermute | solution.py:13
  142.0 22.4 %collective-permute-start.10 = (f32[128,512]{0,1:T(8,128)S(1)}, f32[128,512]{0,1:T(8,128)}, u32[]{:S(2)}, u32[]{:S(2)}) collective-permute-start(f32[128,512]{0,1:T(8,128)S(1)} %convert_add_fusion.4), channel_id=1, source_target_pairs={{1,0},{2,1},{3,2},{4,3},{5,4},{6,5},{7,6},{8,7},{9,8},{10,9},{11,1... | collective-permute-start | bytes 786440 | tf_op jit(solution)/shard_map/ppermute | solution.py:13
  153.8 21.8 %collective-permute-start.15 = (f32[128,512]{0,1:T(8,128)S(1)}, f32[128,512]{0,1:T(8,128)S(1)}, u32[]{:S(2)}, u32[]{:S(2)}) collective-permute-start(f32[128,512]{0,1:T(8,128)S(1)} %convert_add_fusion), channel_id=1, source_target_pairs={{1,0},{2,1},{3,2},{4,3},{5,4},{6,5},{7,6},{8,7},{9,8},{10,9},{11,1... | collective-permute-start | bytes 786440 | tf_op jit(solution)/shard_map/ppermute | solution.py:13
  165.4 14.6 %collective-permute-start.11 = (f32[128,512]{0,1:T(8,128)S(1)}, f32[128,512]{0,1:T(8,128)S(1)}, u32[]{:S(2)}, u32[]{:S(2)}) collective-permute-start(f32[128,512]{0,1:T(8,128)S(1)} %convert_add_fusion.3), channel_id=1, source_target_pairs={{1,0},{2,1},{3,2},{4,3},{5,4},{6,5},{7,6},{8,7},{9,8},{10,9},{11,1... | collective-permute-start | bytes 786440 | tf_op jit(solution)/shard_map/ppermute | solution.py:13
where the time goes:
time: 182 us; the launch traced here: 181 us
  starting transfers between devices  80.6 us (44%)
  waiting for transfers between devices  43.8 us (24%)
  local copies, waits for them, and re-layouts  29.8 us (16%)
  matrix products  20.9 us (11%)
  other arithmetic  4.44 us (2%)
    ppermute x16, starting transfers between devices, passed_along(): return lax.ppermute(shard, axis, pairs)  80.6 us
    ppermute x16, waiting for transfers between devices, passed_along(): return lax.ppermute(shard, axis, pairs)  43.8 us
    unnamed x28, local copies, waits for them, and re-layouts  9.3 us
    slice x1, local copies, waits for them, and re-layouts, head_group(): queries.reshape(tok_rows, -1, query_per_key_head * head_dim)[:, group]  5.32 us
    slice x1, local copies, waits for them, and re-layouts, head_group(): grad_out.reshape(tok_rows, -1, query_per_key_head * head_dim)[:, group]  5.32 us
    dot_general x4, matrix products, head_group(): dprobs = jnp.dot(g_part, v_part.T, preferred_element_type=jnp.float32)  4.16 us
    dot_general x4, matrix products, head_group(): attn_out = jnp.dot(probs_low, v_part, preferred_element_type=jnp.float32)  3.97 us
    dot_general x4, matrix products, head_group(): jnp.dot(probs_low.T, g_part, preferred_element_type=jnp.float32)  3.77 us
  transfers between devices with their start and end apart: 16, of which 8 were waited for; matrix products, arithmetic and copies ran while one was open for 24% of the time, Pallas kernels for 0%

commit v1 on v0

v1 whole, which is shorter than its diff:
```python
import functools

import jax
import jax.numpy as jnp
from jax import lax
from jax.experimental import pallas as pl
from jax.experimental.pallas import tpu as pltpu
from jax.sharding import PartitionSpec as P

HEAD = 128
TOK = 128
SPAN = 4
PER_GROUP = 8
AXES = ("outer", "inner")
F32 = jnp.float32
BF16 = jnp.bfloat16
SCALE = HEAD**-0.5
LOG2E = 1.4426950408889634


def by_parity(x, even, odd):
    peers = lax.axis_size(AXES)
    return lax.ppermute(
        x, AXES, [(i, (i + (odd if i % 2 else even)) % peers) for i in range(peers)]
    )


def with_partner(x):
    peers = lax.axis_size(AXES)
    return lax.ppermute(x, AXES, [(i, i ^ 1) for i in range(peers)])


def rows_by_rows(a, b):
    return lax.dot_general(a, b, (((1,), (1,)), ((), ())), preferred_element_type=F32)


def cols_by_cols(a, b):
    return lax.dot_general(a, b, (((0,), (0,)), ((), ())), preferred_element_type=F32)


def nearest_first(refs, col, odd, count):
    own, both, near, far = refs
    blocks = [own[:, col], both[TOK:, col]]
    if count > 2:
        blocks.append(jnp.where(odd, near[:, col], far[:, col]))
    if count > 3:
        blocks.append(both[:TOK, col])
    if count > 4:
        blocks.append(jnp.where(odd, far[:, col], near[:, col]))
    return jnp.concatenate(blocks, axis=0)


def spread(refs, col, odd, count, x):
    own, both, near, far = refs
    rows = [x[n * TOK : (n + 1) * TOK].astype(BF16) for n in range(count)]
    rows += [jnp.zeros((TOK, HEAD), BF16)] * (SPAN + 1 - count)
    own[:, col] = rows[0]
    both[:, col] = jnp.concatenate([rows[3], rows[1]], axis=0)
    near[:, col] = jnp.where(odd, rows[2], rows[4])
    far[:, col] = jnp.where(odd, rows[4], rows[2])


def heads_stacked(ref):
    return jnp.concatenate([ref[:, h * HEAD : (h + 1) * HEAD] for h in range(PER_GROUP)], axis=0)


def for_each_count(info, attend):
    for count in range(2, SPAN + 2):
        pl.when(info[0] == count)(functools.partial(attend, count))


def probs_kernel(info, starts, q_ref, g_ref, *refs):
    k_refs, p_ref, terms, bias_ref = refs[:4], refs[4], refs[5:9], refs[9]
    i = pl.program_id(0)
    odd = info[1] == 1

    @pl.when(i == 0)
    def _():
        qi = lax.broadcasted_iota(jnp.int32, (TOK, TOK), 1)
        ji = lax.broadcasted_iota(jnp.int32, (TOK, TOK), 0)
        for back in range(SPAN + 1):
            kj = ji - back * TOK
            seen = kj >= starts[...]
            if back == 0:
                seen = seen & (kj <= qi)
            bias_ref[pl.ds(back * TOK, TOK), :] = jnp.where(seen, 0.0, -jnp.inf)

    col = pl.ds(pl.multiple_of(i * HEAD, HEAD), HEAD)

    def attend(count):
        keys = nearest_first(k_refs, col, odd, count)
        bias = jnp.concatenate([bias_ref[: count * TOK, :]] * PER_GROUP, axis=1)
        scores = rows_by_rows(keys, heads_stacked(q_ref)) + bias
        top = jnp.max(scores, axis=0, keepdims=True)
        expo = jnp.exp2((scores - top) * (SCALE * LOG2E))
        low = (expo * (1.0 / jnp.sum(expo, axis=0, keepdims=True))).astype(BF16)
        p_ref[0, : count * TOK, :] = low
        dv = jnp.dot(low, heads_stacked(g_ref), preferred_element_type=F32)
        spread(terms, col, odd, count, dv)

    for_each_count(info, attend)


def scores_kernel(info, q_ref, g_ref, p_ref, *refs):
    k_refs, v_refs, dq_ref, terms = refs[:4], refs[4:8], refs[8], refs[9:13]
    i = pl.program_id(0)
    odd = info[1] == 1
    col = pl.ds(pl.multiple_of(i * HEAD, HEAD), HEAD)

    def attend(count):
        keys = nearest_first(k_refs, col, odd, count)
        vals = nearest_first(v_refs, col, odd, count)
        probs = p_ref[0, : count * TOK, :].astype(F32)
        weighted = probs * rows_by_rows(vals, heads_stacked(g_ref))
        delta = jnp.sum(weighted, axis=0, keepdims=True)
        dscores = (weighted - probs * delta).astype(BF16)
        dk = jnp.dot(dscores, heads_stacked(q_ref), preferred_element_type=F32) * SCALE
        dq = cols_by_cols(keys, dscores) * SCALE
        for h in range(PER_GROUP):
            part = slice(h * HEAD, (h + 1) * HEAD)
            dq_ref[:, part] = dq[:, part].T.astype(BF16)
        spread(terms, col, odd, count, dk)

    for_each_count(info, attend)


def whole(i):
    return (0, 0)


WIDE = pl.BlockSpec((TOK, PER_GROUP * HEAD), lambda i: (0, i))


def call(kernel, name, groups, in_specs, out_specs, out_shape, scratch, *args):
    pairs = TOK * PER_GROUP * TOK * (SPAN + 1) * groups
    return pl.pallas_call(
        kernel,
        grid=(groups,),
        in_specs=in_specs,
        out_specs=out_specs,
        out_shape=out_shape,
        scratch_shapes=scratch,
        compiler_params=pltpu.CompilerParams(vmem_limit_bytes=40 * 2**20),
        cost_estimate=pl.CostEstimate(
            flops=pairs * HEAD * 5, bytes_accessed=2**21, transcendentals=pairs
        ),
        name=name,
    )(*args)


def gathered(own, odd):
    near = by_parity(own, 4, 2)
    far = by_parity(own, 2, 4)
    both = with_partner(jnp.concatenate([far, jnp.where(odd, near, own)], axis=0))
    return [pltpu.with_memory_space_constraint(own, pltpu.HBM), both, near, far]


def returned(own, both, near, far, odd):
    both = with_partner(both).astype(F32)
    far = (far.astype(F32) + both[:TOK]).astype(BF16)
    near = (near.astype(F32) + jnp.where(odd, both[TOK:], 0)).astype(BF16)
    own = own.astype(F32) + jnp.where(odd, 0, both[TOK:])
    far = by_parity(far, -2, -4)
    near = by_parity(near, -4, -2)
    return (own + far.astype(F32) + near.astype(F32)).astype(BF16)


def body(queries, keys, values, grad_out, doc_start):
    groups = keys.shape[1] // HEAD
    queries = pltpu.with_memory_space_constraint(queries, pltpu.HBM)
    grad_out = pltpu.with_memory_space_constraint(grad_out, pltpu.HBM)
    index = lax.axis_index(AXES).astype(jnp.int32)
    odd = index % 2 == 1
    starts = doc_start.reshape(1, TOK) - index * TOK
    reach = (index * TOK - doc_start[0] + TOK - 1) // TOK
    info = jnp.stack([jnp.clip(reach + 1, 2, SPAN + 1), index % 2])
    k_window = gathered(keys, odd)
    v_window = gathered(values, odd)
    blocks = [pl.BlockSpec(x.shape, whole) for x in k_window]
    terms = [jax.ShapeDtypeStruct(x.shape, BF16) for x in k_window]
    width = (SPAN + 1) * TOK
    p_shape = (groups, width, PER_GROUP * TOK)
    p_spec = pl.BlockSpec((1,) + p_shape[1:], lambda i: (i, 0, 0))
    probs, *v_terms = call(
        probs_kernel,
        "probs",
        groups,
        [pl.BlockSpec(memory_space=pltpu.SMEM), pl.BlockSpec((1, TOK), whole), WIDE, WIDE] + blocks,
        [p_spec] + blocks,
        [jax.ShapeDtypeStruct(p_shape, BF16)] + terms,
        [pltpu.VMEM((width, TOK), F32)],
        info,
        starts,
        queries,
        grad_out,
        *k_window,
    )
    grad_queries, *k_terms = call(
        scores_kernel,
        "dscores",
        groups,
        [pl.BlockSpec(memory_space=pltpu.SMEM), WIDE, WIDE, p_spec] + blocks * 2,
        [WIDE] + blocks,
        [jax.ShapeDtypeStruct(queries.shape, BF16)] + terms,
        [],
        info,
        queries,
        grad_out,
        probs,
        *k_window,
        *v_window,
    )
    grad_values = returned(*v_terms, odd)
    grad_keys = returned(*k_terms, odd)
    return grad_queries, grad_keys, grad_values


def solution(mesh):
    rows = P(AXES, None)
    return jax.shard_map(
        body,
        mesh=mesh,
        in_specs=(rows, rows, rows, rows, P(AXES)),
        out_specs=(rows, rows, rows),
        check_vma=False,
    )
```

time: 182 us -> 97.5 us (0.54)
  the two profiles are of different devices: /device:TPU:7 before, /device:TPU:52 now
where the time goes in v1:
time: 97.5 us; the launch traced here: 96.8 us
  starting transfers between devices  57 us (58%)
  waiting for transfers between devices  22.9 us (23%)
  Pallas kernels  11.1 us (11%)
  other arithmetic  4.33 us (4%)
  between operations  1.5 us (2%)
    ppermute x8, starting transfers between devices, by_parity(): lax.ppermute(x, AXES, [(i, (i + (odd if i % 2 else even)) % peers) for i...  45.4 us
    ppermute x8, waiting for transfers between devices, by_parity(): lax.ppermute(x, AXES, [(i, (i + (odd if i % 2 else even)) % peers) for i...  22.9 us
    ppermute x4, starting transfers between devices, with_partner(): return lax.ppermute(x, AXES, [(i, i ^ 1) for i in range(peers)])  11.6 us
    pallas_call x2, Pallas kernels, call(): pl.pallas_call(kernel, grid=(groups,), in_specs=in_specs, out_specs=out_s...  11.1 us
  transfers between devices with their start and end apart: 12, of which 4 were waited for; matrix products, arithmetic and copies ran while one was open for 4% of the time, Pallas kernels for 11%

profile of v1, /device:TPU:52, one launch (start us, length us, event | category | flops | bytes accessed | tf_op | source)
XLA Modules:
  0.0 96.8 jit_solution(4267786411064928189)
XLA Ops:
  0.6 10.9 %collective-permute-start.1 = (bf16[128,512]{1,0:T(8,128)(2,1)}, bf16[128,512]{1,0:T(8,128)(2,1)S(1)}, u32[]{:S(2)}, u32[]{:S(2)}) collective-permute-start(bf16[128,512]{1,0:T(8,128)(2,1)} %refs_0_.3), channel_id=1, source_target_pairs={{0,4},{1,3},{2,6},{3,5},{4,8},{5,7},{6,10},{7,9},{8,12},{9,11},{10... | collective-permute-start | bytes 393224 | tf_op jit(solution)/shard_map/ppermute | solution.py:23
  11.6 4.3 %collective-permute-start = (bf16[128,512]{1,0:T(8,128)(2,1)}, bf16[128,512]{1,0:T(8,128)(2,1)S(1)}, u32[]{:S(2)}, u32[]{:S(2)}) collective-permute-start(bf16[128,512]{1,0:T(8,128)(2,1)} %refs_0_.3), channel_id=1, source_target_pairs={{0,2},{1,5},{2,4},{3,7},{4,6},{5,9},{6,8},{7,11},{8,10},{9,13},{10... | collective-permute-start | bytes 393224 | tf_op jit(solution)/shard_map/ppermute | solution.py:23
  15.9 1.9 %collective-permute-start.4 = (bf16[128,512]{1,0:T(8,128)(2,1)}, bf16[128,512]{1,0:T(8,128)(2,1)S(1)}, u32[]{:S(2)}, u32[]{:S(2)}) collective-permute-start(bf16[128,512]{1,0:T(8,128)(2,1)} %refs_4_.1), channel_id=1, source_target_pairs={{0,4},{1,3},{2,6},{3,5},{4,8},{5,7},{6,10},{7,9},{8,12},{9,11},{10... | collective-permute-start | bytes 393224 | tf_op jit(solution)/shard_map/ppermute | solution.py:23
  17.8 4.5 %collective-permute-start.3 = (bf16[128,512]{1,0:T(8,128)(2,1)}, bf16[128,512]{1,0:T(8,128)(2,1)S(1)}, u32[]{:S(2)}, u32[]{:S(2)}) collective-permute-start(bf16[128,512]{1,0:T(8,128)(2,1)} %refs_4_.1), channel_id=1, source_target_pairs={{0,2},{1,5},{2,4},{3,7},{4,6},{5,9},{6,8},{7,11},{8,10},{9,13},{10... | collective-permute-start | bytes 393224 | tf_op jit(solution)/shard_map/ppermute | solution.py:23
  23.0 0.7 subtract_bitcast_fusion.starts
  23.6 0.0 collective-permute-done.1.refs_2_
  23.6 0.9 broadcast_select_fusion.1
  24.6 2.7 %collective-permute-done.refs_3_ = bf16[128,512]{1,0:T(8,128)(2,1)S(1)} collective-permute-done((bf16[128,512]{1,0:T(8,128)(2,1)}, bf16[128,512]{1,0:T(8,128)(2,1)S(1)}, u32[]{:S(2)}, u32[]{:S(2)}) %collective-permute-start) | collective-permute-done | bytes 131104 | tf_op jit(solution)/shard_map/ppermute | solution.py:23
  27.3 1.9 %collective-permute-start.2 = (bf16[256,512]{1,0:T(8,128)(2,1)S(1)}, bf16[256,512]{1,0:T(8,128)(2,1)S(1)}, u32[]{:S(2)}, u32[]{:S(2)}) collective-permute-start(bf16[256,512]{1,0:T(8,128)(2,1)S(1)} %pad_maximum_fusion), channel_id=1, source_target_pairs={{0,1},{1,0},{2,3},{3,2},{4,5},{5,4},{6,7},{7,6},{8,9},{9,8},{10,11... | collective-permute-start | bytes 786440 | tf_op jit(solution)/shard_map/ppermute | solution.py:30
  29.3 3.9 %collective-permute-done.4.refs_6_ = bf16[128,512]{1,0:T(8,128)(2,1)S(1)} collective-permute-done((bf16[128,512]{1,0:T(8,128)(2,1)}, bf16[128,512]{1,0:T(8,128)(2,1)S(1)}, u32[]{:S(2)}, u32[]{:S(2)}) %collective-permute-start.4) | collective-permute-done | bytes 131104 | tf_op jit(solution)/shard_map/ppermute | solution.py:23
  33.1 0.9 broadcast_select_fusion
  34.1 4.7 %collective-permute-done.3.refs_7_ = bf16[128,512]{1,0:T(8,128)(2,1)S(1)} collective-permute-done((bf16[128,512]{1,0:T(8,128)(2,1)}, bf16[128,512]{1,0:T(8,128)(2,1)S(1)}, u32[]{:S(2)}, u32[]{:S(2)}) %collective-permute-start.3) | collective-permute-done | bytes 131104 | tf_op jit(solution)/shard_map/ppermute | solution.py:23
  38.7 1.9 %collective-permute-start.5 = (bf16[256,512]{1,0:T(8,128)(2,1)S(1)}, bf16[256,512]{1,0:T(8,128)(2,1)S(1)}, u32[]{:S(2)}, u32[]{:S(2)}) collective-permute-start(bf16[256,512]{1,0:T(8,128)(2,1)S(1)} %pad_maximum_fusion.1), channel_id=1, source_target_pairs={{0,1},{1,0},{2,3},{3,2},{4,5},{5,4},{6,7},{7,6},{8,9},{9,8},{10,11... | collective-permute-start | bytes 786440 | tf_op jit(solution)/shard_map/ppermute | solution.py:30
  40.7 0.1 pad_add_fusion.info
  40.7 0.0 collective-permute-done.2.refs_1_
  40.7 5.3 %probs.1 = (bf16[4,640,1024]{2,1,0:T(8,128)(2,1)S(1)}, bf16[128,512]{1,0:T(8,128)(2,1)S(1)}, bf16[256,512]{1,0:T(8,128)(2,1)S(1)}, bf16[128,512]{1,0:T(8,128)(2,1)S(1)}, bf16[128,512]{1,0:T(8,128)(2,1)S(1)}) custom-call(s32[2]{0:T(128)S(1)} %pad_add_fusion.info, s32[1,128]{1,0:T(1,128)S(1)} %subtract_bitcast_fusion.starts, bf16[128,4096]{1,0:T(8,128)(2,1)} %q_ref.3, ...), custom_call_target="tpu_custom_call" | custom-call | flops 1677721600 | bytes 2097152 | tf_op jit(solution)/shard_map/probs/pallas_call | solution.py:136
  46.0 5.0 %collective-permute-start.9 = (bf16[256,512]{1,0:T(8,128)(2,1)S(1)}, bf16[256,512]{1,0:T(8,128)(2,1)S(1)}, u32[]{:S(2)}, u32[]{:S(2)}) collective-permute-start(bf16[256,512]{1,0:T(8,128)(2,1)S(1)} %get-tuple-element.20), channel_id=1, source_target_pairs={{0,1},{1,0},{2,3},{3,2},{4,5},{5,4},{6,7},{7,6},{8,9},{9,8},{10,11... | collective-permute-start | bytes 786440 | tf_op jit(solution)/shard_map/ppermute | solution.py:30
  51.0 0.0 collective-permute-done.5.refs_5_
  51.0 5.9 %dscores.1 = (bf16[128,4096]{1,0:T(8,128)(2,1)}, bf16[128,512]{1,0:T(8,128)(2,1)S(1)}, bf16[256,512]{1,0:T(8,128)(2,1)S(1)}, bf16[128,512]{1,0:T(8,128)(2,1)S(1)}, bf16[128,512]{1,0:T(8,128)(2,1)S(1)}) custom-call(s32[2]{0:T(128)S(1)} %pad_add_fusion.info, bf16[128,4096]{1,0:T(8,128)(2,1)} %q_ref.3, bf16[128,4096]{1,0:T(8,128)(2,1)} %g_ref.3, ...), custom_call_target="tpu_custom_call" | custom-call | flops 1677721600 | bytes 2097152 | tf_op jit(solution)/shard_map/dscores/pallas_call | solution.py:136
  56.9 2.8 %collective-permute-start.6 = (bf16[256,512]{1,0:T(8,128)(2,1)S(1)}, bf16[256,512]{1,0:T(8,128)(2,1)S(1)}, u32[]{:S(2)}, u32[]{:S(2)}) collective-permute-start(bf16[256,512]{1,0:T(8,128)(2,1)S(1)} %get-tuple-element.16), channel_id=1, source_target_pairs={{0,1},{1,0},{2,3},{3,2},{4,5},{5,4},{6,7},{7,6},{8,9},{9,8},{10,11... | collective-permute-start | bytes 786440 | tf_op jit(solution)/shard_map/ppermute | solution.py:30
  59.7 0.0 collective-permute-done.9
  59.7 0.1 convert_element_type.70
  59.7 0.1 fusion
  59.8 3.7 %collective-permute-start.10 = (bf16[128,512]{1,0:T(8,128)(2,1)S(1)}, bf16[128,512]{1,0:T(8,128)(2,1)S(1)}, u32[]{:S(2)}, u32[]{:S(2)}) collective-permute-start(bf16[128,512]{1,0:T(8,128)(2,1)S(1)} %get-tuple-element.23), channel_id=1, source_target_pairs={{0,510},{1,509},{2,0},{3,511},{4,2},{5,1},{6,4},{7,3},{8,6},{9,5},... | collective-permute-start | bytes 393224 | tf_op jit(solution)/shard_map/ppermute | solution.py:23
  63.5 6.5 %collective-permute-start.11 = (bf16[128,512]{1,0:T(8,128)(2,1)S(1)}, bf16[128,512]{1,0:T(8,128)(2,1)S(1)}, u32[]{:S(2)}, u32[]{:S(2)}) collective-permute-start(bf16[128,512]{1,0:T(8,128)(2,1)S(1)} %get-tuple-element.24), channel_id=1, source_target_pairs={{0,508},{1,511},{2,510},{3,1},{4,0},{5,3},{6,2},{7,5},{8,4},{9,7},... | collective-permute-start | bytes 393224 | tf_op jit(solution)/shard_map/ppermute | solution.py:23
  70.0 0.0 collective-permute-done.6
  70.0 0.1 convert_element_type.61
  70.1 0.1 fusion.1
  70.2 1.9 %collective-permute-start.7 = (bf16[128,512]{1,0:T(8,128)(2,1)S(1)}, bf16[128,512]{1,0:T(8,128)(2,1)S(1)}, u32[]{:S(2)}, u32[]{:S(2)}) collective-permute-start(bf16[128,512]{1,0:T(8,128)(2,1)S(1)} %get-tuple-element.25), channel_id=1, source_target_pairs={{0,510},{1,509},{2,0},{3,511},{4,2},{5,1},{6,4},{7,3},{8,6},{9,5},... | collective-permute-start | bytes 393224 | tf_op jit(solution)/shard_map/ppermute | solution.py:23
  72.1 11.7 %collective-permute-start.8 = (bf16[128,512]{1,0:T(8,128)(2,1)S(1)}, bf16[128,512]{1,0:T(8,128)(2,1)S(1)}, u32[]{:S(2)}, u32[]{:S(2)}) collective-permute-start(bf16[128,512]{1,0:T(8,128)(2,1)S(1)} %get-tuple-element.26), channel_id=1, source_target_pairs={{0,508},{1,511},{2,510},{3,1},{4,0},{5,3},{6,2},{7,5},{8,4},{9,7},... | collective-permute-start | bytes 393224 | tf_op jit(solution)/shard_map/ppermute | solution.py:23
  83.8 0.0 collective-permute-done.10
  83.8 0.0 collective-permute-done.11
  83.8 0.7 add_convert_fusion
  84.6 11.6 %collective-permute-done.7 = bf16[128,512]{1,0:T(8,128)(2,1)S(1)} collective-permute-done((bf16[128,512]{1,0:T(8,128)(2,1)S(1)}, bf16[128,512]{1,0:T(8,128)(2,1)S(1)}, u32[]{:S(2)}, u32[]{:S(2)}) %collective-permute-start.7) | collective-permute-done | bytes 131104 | tf_op jit(solution)/shard_map/ppermute | solution.py:23
  96.1 0.0 collective-permute-done.8
  96.1 0.7 add_convert_fusion.2
  (2 shorter events, 0.0 us)
Async XLA Ops:
  0.6 23.0 %collective-permute-start.1 = (bf16[128,512]{1,0:T(8,128)(2,1)}, bf16[128,512]{1,0:T(8,128)(2,1)S(1)}, u32[]{:S(2)}, u32[]{:S(2)}) collective-permute-start(bf16[128,512]{1,0:T(8,128)(2,1)} %refs_0_.3), channel_id=1, source_target_pairs={{0,4},{1,3},{2,6},{3,5},{4,8},{5,7},{6,10},{7,9},{8,12},{9,11},{10... | collective-permute-start | bytes 393224 | tf_op jit(solution)/shard_map/ppermute | solution.py:23
  11.6 15.8 %collective-permute-start = (bf16[128,512]{1,0:T(8,128)(2,1)}, bf16[128,512]{1,0:T(8,128)(2,1)S(1)}, u32[]{:S(2)}, u32[]{:S(2)}) collective-permute-start(bf16[128,512]{1,0:T(8,128)(2,1)} %refs_0_.3), channel_id=1, source_target_pairs={{0,2},{1,5},{2,4},{3,7},{4,6},{5,9},{6,8},{7,11},{8,10},{9,13},{10... | collective-permute-start | bytes 393224 | tf_op jit(solution)/shard_map/ppermute | solution.py:23
  15.9 17.3 %collective-permute-start.4 = (bf16[128,512]{1,0:T(8,128)(2,1)}, bf16[128,512]{1,0:T(8,128)(2,1)S(1)}, u32[]{:S(2)}, u32[]{:S(2)}) collective-permute-start(bf16[128,512]{1,0:T(8,128)(2,1)} %refs_4_.1), channel_id=1, source_target_pairs={{0,4},{1,3},{2,6},{3,5},{4,8},{5,7},{6,10},{7,9},{8,12},{9,11},{10... | collective-permute-start | bytes 393224 | tf_op jit(solution)/shard_map/ppermute | solution.py:23
  17.8 20.9 %collective-permute-start.3 = (bf16[128,512]{1,0:T(8,128)(2,1)}, bf16[128,512]{1,0:T(8,128)(2,1)S(1)}, u32[]{:S(2)}, u32[]{:S(2)}) collective-permute-start(bf16[128,512]{1,0:T(8,128)(2,1)} %refs_4_.1), channel_id=1, source_target_pairs={{0,2},{1,5},{2,4},{3,7},{4,6},{5,9},{6,8},{7,11},{8,10},{9,13},{10... | collective-permute-start | bytes 393224 | tf_op jit(solution)/shard_map/ppermute | solution.py:23
  27.3 13.4 %collective-permute-start.2 = (bf16[256,512]{1,0:T(8,128)(2,1)S(1)}, bf16[256,512]{1,0:T(8,128)(2,1)S(1)}, u32[]{:S(2)}, u32[]{:S(2)}) collective-permute-start(bf16[256,512]{1,0:T(8,128)(2,1)S(1)} %pad_maximum_fusion), channel_id=1, source_target_pairs={{0,1},{1,0},{2,3},{3,2},{4,5},{5,4},{6,7},{7,6},{8,9},{9,8},{10,11... | collective-permute-start | bytes 786440 | tf_op jit(solution)/shard_map/ppermute | solution.py:30
  38.7 12.3 %collective-permute-start.5 = (bf16[256,512]{1,0:T(8,128)(2,1)S(1)}, bf16[256,512]{1,0:T(8,128)(2,1)S(1)}, u32[]{:S(2)}, u32[]{:S(2)}) collective-permute-start(bf16[256,512]{1,0:T(8,128)(2,1)S(1)} %pad_maximum_fusion.1), channel_id=1, source_target_pairs={{0,1},{1,0},{2,3},{3,2},{4,5},{5,4},{6,7},{7,6},{8,9},{9,8},{10,11... | collective-permute-start | bytes 786440 | tf_op jit(solution)/shard_map/ppermute | solution.py:30
  46.0 13.7 %collective-permute-start.9 = (bf16[256,512]{1,0:T(8,128)(2,1)S(1)}, bf16[256,512]{1,0:T(8,128)(2,1)S(1)}, u32[]{:S(2)}, u32[]{:S(2)}) collective-permute-start(bf16[256,512]{1,0:T(8,128)(2,1)S(1)} %get-tuple-element.20), channel_id=1, source_target_pairs={{0,1},{1,0},{2,3},{3,2},{4,5},{5,4},{6,7},{7,6},{8,9},{9,8},{10,11... | collective-permute-start | bytes 786440 | tf_op jit(solution)/shard_map/ppermute | solution.py:30
  56.9 13.1 %collective-permute-start.6 = (bf16[256,512]{1,0:T(8,128)(2,1)S(1)}, bf16[256,512]{1,0:T(8,128)(2,1)S(1)}, u32[]{:S(2)}, u32[]{:S(2)}) collective-permute-start(bf16[256,512]{1,0:T(8,128)(2,1)S(1)} %get-tuple-element.16), channel_id=1, source_target_pairs={{0,1},{1,0},{2,3},{3,2},{4,5},{5,4},{6,7},{7,6},{8,9},{9,8},{10,11... | collective-permute-start | bytes 786440 | tf_op jit(solution)/shard_map/ppermute | solution.py:30
  59.8 24.0 %collective-permute-start.10 = (bf16[128,512]{1,0:T(8,128)(2,1)S(1)}, bf16[128,512]{1,0:T(8,128)(2,1)S(1)}, u32[]{:S(2)}, u32[]{:S(2)}) collective-permute-start(bf16[128,512]{1,0:T(8,128)(2,1)S(1)} %get-tuple-element.23), channel_id=1, source_target_pairs={{0,510},{1,509},{2,0},{3,511},{4,2},{5,1},{6,4},{7,3},{8,6},{9,5},... | collective-permute-start | bytes 393224 | tf_op jit(solution)/shard_map/ppermute | solution.py:23
  63.5 20.3 %collective-permute-start.11 = (bf16[128,512]{1,0:T(8,128)(2,1)S(1)}, bf16[128,512]{1,0:T(8,128)(2,1)S(1)}, u32[]{:S(2)}, u32[]{:S(2)}) collective-permute-start(bf16[128,512]{1,0:T(8,128)(2,1)S(1)} %get-tuple-element.24), channel_id=1, source_target_pairs={{0,508},{1,511},{2,510},{3,1},{4,0},{5,3},{6,2},{7,5},{8,4},{9,7},... | collective-permute-start | bytes 393224 | tf_op jit(solution)/shard_map/ppermute | solution.py:23
  70.2 25.9 %collective-permute-start.7 = (bf16[128,512]{1,0:T(8,128)(2,1)S(1)}, bf16[128,512]{1,0:T(8,128)(2,1)S(1)}, u32[]{:S(2)}, u32[]{:S(2)}) collective-permute-start(bf16[128,512]{1,0:T(8,128)(2,1)S(1)} %get-tuple-element.25), channel_id=1, source_target_pairs={{0,510},{1,509},{2,0},{3,511},{4,2},{5,1},{6,4},{7,3},{8,6},{9,5},... | collective-permute-start | bytes 393224 | tf_op jit(solution)/shard_map/ppermute | solution.py:23
  72.1 24.0 %collective-permute-start.8 = (bf16[128,512]{1,0:T(8,128)(2,1)S(1)}, bf16[128,512]{1,0:T(8,128)(2,1)S(1)}, u32[]{:S(2)}, u32[]{:S(2)}) collective-permute-start(bf16[128,512]{1,0:T(8,128)(2,1)S(1)} %get-tuple-element.26), channel_id=1, source_target_pairs={{0,508},{1,511},{2,510},{3,1},{4,0},{5,3},{6,2},{7,5},{8,4},{9,7},... | collective-permute-start | bytes 393224 | tf_op jit(solution)/shard_map/ppermute | solution.py:23

commit v2 on v1

--- a/solution.py
+++ b/solution.py
@@ -152,7 +152,7 @@
     near = by_parity(own, 4, 2)
     far = by_parity(own, 2, 4)
     both = with_partner(jnp.concatenate([far, jnp.where(odd, near, own)], axis=0))
-    return [pltpu.with_memory_space_constraint(own, pltpu.HBM), both, near, far]
+    return [own, both, near, far]
 
 
 def returned(own, both, near, far, odd):
@@ -167,8 +167,6 @@
 
 def body(queries, keys, values, grad_out, doc_start):
     groups = keys.shape[1] // HEAD
-    queries = pltpu.with_memory_space_constraint(queries, pltpu.HBM)
-    grad_out = pltpu.with_memory_space_constraint(grad_out, pltpu.HBM)
     index = lax.axis_index(AXES).astype(jnp.int32)
     odd = index % 2 == 1
     starts = doc_start.reshape(1, TOK) - index * TOK
@@ -191,9 +189,10 @@
         [pltpu.VMEM((width, TOK), F32)],
         info,
         starts,
-        queries,
-        grad_out,
-        *k_window,
+        pltpu.with_memory_space_constraint(queries, pltpu.HBM),
+        pltpu.with_memory_space_constraint(grad_out, pltpu.HBM),
+        pltpu.with_memory_space_constraint(k_window[0], pltpu.HBM),
+        *k_window[1:],
     )
     grad_queries, *k_terms = call(
         scores_kernel,

time: 97.5 us -> 96.9 us (level)
  the two profiles are of different devices: /device:TPU:52 before, /device:TPU:15 now
where the time goes in v2:
time: 96.9 us; the launch traced here: 96.8 us
  starting transfers between devices  62.3 us (64%)
  waiting for transfers between devices  19.3 us (20%)
  Pallas kernels  9.34 us (10%)
  other arithmetic  4.34 us (4%)
  between operations  1.56 us (2%)
    ppermute x8, starting transfers between devices, by_parity(): lax.ppermute(x, AXES, [(i, (i + (odd if i % 2 else even)) % peers) for i...  53.2 us
    ppermute x8, waiting for transfers between devices, by_parity(): lax.ppermute(x, AXES, [(i, (i + (odd if i % 2 else even)) % peers) for i...  19.3 us
    pallas_call x2, Pallas kernels, call(): pl.pallas_call(kernel, grid=(groups,), in_specs=in_specs, out_specs=out_s...  9.34 us
    ppermute x4, starting transfers between devices, with_partner(): return lax.ppermute(x, AXES, [(i, i ^ 1) for i in range(peers)])  9.11 us
  transfers between devices with their start and end apart: 12, of which 5 were waited for; matrix products, arithmetic and copies ran while one was open for 4% of the time, Pallas kernels for 10%

profile of v2, /device:TPU:15, one launch (start us, length us, event | category | flops | bytes accessed | tf_op | source)
XLA Modules:
  0.0 96.8 jit_solution(8237823431848957669)
XLA Ops:
  0.6 0.0 copy-start.2
  0.6 0.0 copy-start.3
  0.7 0.0 copy-start
  0.7 0.0 copy-start.1
  0.7 10.8 %collective-permute-start.1 = (bf16[128,512]{1,0:T(8,128)(2,1)}, bf16[128,512]{1,0:T(8,128)(2,1)S(1)}, u32[]{:S(2)}, u32[]{:S(2)}) collective-permute-start(bf16[128,512]{1,0:T(8,128)(2,1)} %refs_0_.3), channel_id=1, source_target_pairs={{0,4},{1,3},{2,6},{3,5},{4,8},{5,7},{6,10},{7,9},{8,12},{9,11},{10... | collective-permute-start | bytes 393224 | tf_op jit(solution)/shard_map/ppermute | solution.py:23
  11.5 4.0 %collective-permute-start = (bf16[128,512]{1,0:T(8,128)(2,1)}, bf16[128,512]{1,0:T(8,128)(2,1)S(1)}, u32[]{:S(2)}, u32[]{:S(2)}) collective-permute-start(bf16[128,512]{1,0:T(8,128)(2,1)} %refs_0_.3), channel_id=1, source_target_pairs={{0,2},{1,5},{2,4},{3,7},{4,6},{5,9},{6,8},{7,11},{8,10},{9,13},{10... | collective-permute-start | bytes 393224 | tf_op jit(solution)/shard_map/ppermute | solution.py:23
  15.5 2.4 %collective-permute-start.4 = (bf16[128,512]{1,0:T(8,128)(2,1)}, bf16[128,512]{1,0:T(8,128)(2,1)S(1)}, u32[]{:S(2)}, u32[]{:S(2)}) collective-permute-start(bf16[128,512]{1,0:T(8,128)(2,1)} %refs_4_.1), channel_id=1, source_target_pairs={{0,4},{1,3},{2,6},{3,5},{4,8},{5,7},{6,10},{7,9},{8,12},{9,11},{10... | collective-permute-start | bytes 393224 | tf_op jit(solution)/shard_map/ppermute | solution.py:23
  17.9 7.0 %collective-permute-start.3 = (bf16[128,512]{1,0:T(8,128)(2,1)}, bf16[128,512]{1,0:T(8,128)(2,1)S(1)}, u32[]{:S(2)}, u32[]{:S(2)}) collective-permute-start(bf16[128,512]{1,0:T(8,128)(2,1)} %refs_4_.1), channel_id=1, source_target_pairs={{0,2},{1,5},{2,4},{3,7},{4,6},{5,9},{6,8},{7,11},{8,10},{9,13},{10... | collective-permute-start | bytes 393224 | tf_op jit(solution)/shard_map/ppermute | solution.py:23
  25.6 0.7 subtract_bitcast_fusion.starts
  26.2 0.0 collective-permute-done.1.refs_2_
  26.2 0.9 broadcast_select_fusion.1
  27.2 6.7 %collective-permute-done.refs_3_ = bf16[128,512]{1,0:T(8,128)(2,1)S(1)} collective-permute-done((bf16[128,512]{1,0:T(8,128)(2,1)}, bf16[128,512]{1,0:T(8,128)(2,1)S(1)}, u32[]{:S(2)}, u32[]{:S(2)}) %collective-permute-start) | collective-permute-done | bytes 131104 | tf_op jit(solution)/shard_map/ppermute | solution.py:23
  33.8 1.9 %collective-permute-start.2 = (bf16[256,512]{1,0:T(8,128)(2,1)S(1)}, bf16[256,512]{1,0:T(8,128)(2,1)S(1)}, u32[]{:S(2)}, u32[]{:S(2)}) collective-permute-start(bf16[256,512]{1,0:T(8,128)(2,1)S(1)} %pad_maximum_fusion), channel_id=1, source_target_pairs={{0,1},{1,0},{2,3},{3,2},{4,5},{5,4},{6,7},{7,6},{8,9},{9,8},{10,11... | collective-permute-start | bytes 786440 | tf_op jit(solution)/shard_map/ppermute | solution.py:30
  35.8 0.3 collective-permute-done.4.refs_6_
  36.1 0.9 broadcast_select_fusion
  37.0 4.6 %collective-permute-done.3.refs_7_ = bf16[128,512]{1,0:T(8,128)(2,1)S(1)} collective-permute-done((bf16[128,512]{1,0:T(8,128)(2,1)}, bf16[128,512]{1,0:T(8,128)(2,1)S(1)}, u32[]{:S(2)}, u32[]{:S(2)}) %collective-permute-start.3) | collective-permute-done | bytes 131104 | tf_op jit(solution)/shard_map/ppermute | solution.py:23
  41.7 1.9 %collective-permute-start.5 = (bf16[256,512]{1,0:T(8,128)(2,1)S(1)}, bf16[256,512]{1,0:T(8,128)(2,1)S(1)}, u32[]{:S(2)}, u32[]{:S(2)}) collective-permute-start(bf16[256,512]{1,0:T(8,128)(2,1)S(1)} %pad_maximum_fusion.1), channel_id=1, source_target_pairs={{0,1},{1,0},{2,3},{3,2},{4,5},{5,4},{6,7},{7,6},{8,9},{9,8},{10,11... | collective-permute-start | bytes 786440 | tf_op jit(solution)/shard_map/ppermute | solution.py:30
  43.6 0.1 pad_add_fusion.info
  43.7 0.0 collective-permute-done.2.refs_1_
  43.7 4.5 %probs.1 = (bf16[4,640,1024]{2,1,0:T(8,128)(2,1)S(1)}, bf16[128,512]{1,0:T(8,128)(2,1)S(1)}, bf16[256,512]{1,0:T(8,128)(2,1)S(1)}, bf16[128,512]{1,0:T(8,128)(2,1)S(1)}, bf16[128,512]{1,0:T(8,128)(2,1)S(1)}) custom-call(s32[2]{0:T(128)S(1)} %pad_add_fusion.info, s32[1,128]{1,0:T(1,128)S(1)} %subtract_bitcast_fusion.starts, bf16[128,4096]{1,0:T(8,128)(2,1)} %q_ref.3, ...), custom_call_target="tpu_custom_call" | custom-call | flops 1677721600 | bytes 2097152 | tf_op jit(solution)/shard_map/probs/pallas_call | solution.py:136
  48.2 3.4 %collective-permute-start.9 = (bf16[256,512]{1,0:T(8,128)(2,1)S(1)}, bf16[256,512]{1,0:T(8,128)(2,1)S(1)}, u32[]{:S(2)}, u32[]{:S(2)}) collective-permute-start(bf16[256,512]{1,0:T(8,128)(2,1)S(1)} %get-tuple-element.20), channel_id=1, source_target_pairs={{0,1},{1,0},{2,3},{3,2},{4,5},{5,4},{6,7},{7,6},{8,9},{9,8},{10,11... | collective-permute-start | bytes 786440 | tf_op jit(solution)/shard_map/ppermute | solution.py:30
  51.6 0.0 collective-permute-done.5.refs_5_
  51.6 0.0 copy-done.2
  51.6 0.0 copy-done.3
  51.6 0.0 copy-done
  51.6 0.0 copy-done.1
  51.6 4.8 %dscores.1 = (bf16[128,4096]{1,0:T(8,128)(2,1)}, bf16[128,512]{1,0:T(8,128)(2,1)S(1)}, bf16[256,512]{1,0:T(8,128)(2,1)S(1)}, bf16[128,512]{1,0:T(8,128)(2,1)S(1)}, bf16[128,512]{1,0:T(8,128)(2,1)S(1)}) custom-call(s32[2]{0:T(128)S(1)} %pad_add_fusion.info, bf16[128,4096]{1,0:T(8,128)(2,1)S(1)} %copy-done, bf16[128,4096]{1,0:T(8,128)(2,1)S(1)} %copy-done.1, ...), custom_call_target="tpu_custom_call" | custom-call | flops 1677721600 | bytes 2097152 | tf_op jit(solution)/shard_map/dscores/pallas_call | solution.py:136
  56.4 1.9 %collective-permute-start.6 = (bf16[256,512]{1,0:T(8,128)(2,1)S(1)}, bf16[256,512]{1,0:T(8,128)(2,1)S(1)}, u32[]{:S(2)}, u32[]{:S(2)}) collective-permute-start(bf16[256,512]{1,0:T(8,128)(2,1)S(1)} %get-tuple-element.16), channel_id=1, source_target_pairs={{0,1},{1,0},{2,3},{3,2},{4,5},{5,4},{6,7},{7,6},{8,9},{9,8},{10,11... | collective-permute-start | bytes 786440 | tf_op jit(solution)/shard_map/ppermute | solution.py:30
  58.4 0.0 collective-permute-done.9
  58.4 0.1 convert_element_type.70
  58.4 0.1 fusion
  58.5 14.4 %collective-permute-start.10 = (bf16[128,512]{1,0:T(8,128)(2,1)S(1)}, bf16[128,512]{1,0:T(8,128)(2,1)S(1)}, u32[]{:S(2)}, u32[]{:S(2)}) collective-permute-start(bf16[128,512]{1,0:T(8,128)(2,1)S(1)} %get-tuple-element.23), channel_id=1, source_target_pairs={{0,510},{1,509},{2,0},{3,511},{4,2},{5,1},{6,4},{7,3},{8,6},{9,5},... | collective-permute-start | bytes 393224 | tf_op jit(solution)/shard_map/ppermute | solution.py:23
  72.9 1.9 %collective-permute-start.11 = (bf16[128,512]{1,0:T(8,128)(2,1)S(1)}, bf16[128,512]{1,0:T(8,128)(2,1)S(1)}, u32[]{:S(2)}, u32[]{:S(2)}) collective-permute-start(bf16[128,512]{1,0:T(8,128)(2,1)S(1)} %get-tuple-element.24), channel_id=1, source_target_pairs={{0,508},{1,511},{2,510},{3,1},{4,0},{5,3},{6,2},{7,5},{8,4},{9,7},... | collective-permute-start | bytes 393224 | tf_op jit(solution)/shard_map/ppermute | solution.py:23
  74.8 0.0 collective-permute-done.6
  74.8 0.1 convert_element_type.61
  74.9 0.1 fusion.1
  75.0 10.8 %collective-permute-start.7 = (bf16[128,512]{1,0:T(8,128)(2,1)S(1)}, bf16[128,512]{1,0:T(8,128)(2,1)S(1)}, u32[]{:S(2)}, u32[]{:S(2)}) collective-permute-start(bf16[128,512]{1,0:T(8,128)(2,1)S(1)} %get-tuple-element.25), channel_id=1, source_target_pairs={{0,510},{1,509},{2,0},{3,511},{4,2},{5,1},{6,4},{7,3},{8,6},{9,5},... | collective-permute-start | bytes 393224 | tf_op jit(solution)/shard_map/ppermute | solution.py:23
  85.8 1.9 %collective-permute-start.8 = (bf16[128,512]{1,0:T(8,128)(2,1)S(1)}, bf16[128,512]{1,0:T(8,128)(2,1)S(1)}, u32[]{:S(2)}, u32[]{:S(2)}) collective-permute-start(bf16[128,512]{1,0:T(8,128)(2,1)S(1)} %get-tuple-element.26), channel_id=1, source_target_pairs={{0,508},{1,511},{2,510},{3,1},{4,0},{5,3},{6,2},{7,5},{8,4},{9,7},... | collective-permute-start | bytes 393224 | tf_op jit(solution)/shard_map/ppermute | solution.py:23
  87.7 0.0 collective-permute-done.10
  87.7 0.0 collective-permute-done.11
  87.7 0.7 add_convert_fusion
  88.4 1.7 %collective-permute-done.7 = bf16[128,512]{1,0:T(8,128)(2,1)S(1)} collective-permute-done((bf16[128,512]{1,0:T(8,128)(2,1)S(1)}, bf16[128,512]{1,0:T(8,128)(2,1)S(1)}, u32[]{:S(2)}, u32[]{:S(2)}) %collective-permute-start.7) | collective-permute-done | bytes 131104 | tf_op jit(solution)/shard_map/ppermute | solution.py:23
  90.1 6.0 %collective-permute-done.8 = bf16[128,512]{1,0:T(8,128)(2,1)S(1)} collective-permute-done((bf16[128,512]{1,0:T(8,128)(2,1)S(1)}, bf16[128,512]{1,0:T(8,128)(2,1)S(1)}, u32[]{:S(2)}, u32[]{:S(2)}) %collective-permute-start.8) | collective-permute-done | bytes 131104 | tf_op jit(solution)/shard_map/ppermute | solution.py:23
  96.1 0.7 add_convert_fusion.2
  (2 shorter events, 0.0 us)
Async XLA Ops:
  0.6 51.0 %copy-start.2 = (bf16[128,512]{1,0:T(8,128)(2,1)S(1)}, bf16[128,512]{1,0:T(8,128)(2,1)}, u32[]{:S(2)}) copy-start(bf16[128,512]{1,0:T(8,128)(2,1)} %refs_0_.3) | copy-start | bytes 393220
  0.6 51.0 %copy-start.3 = (bf16[128,512]{1,0:T(8,128)(2,1)S(1)}, bf16[128,512]{1,0:T(8,128)(2,1)}, u32[]{:S(2)}) copy-start(bf16[128,512]{1,0:T(8,128)(2,1)} %refs_4_.1) | copy-start | bytes 393220
  0.7 51.0 %copy-start = (bf16[128,4096]{1,0:T(8,128)(2,1)S(1)}, bf16[128,4096]{1,0:T(8,128)(2,1)}, u32[]{:S(2)}) copy-start(bf16[128,4096]{1,0:T(8,128)(2,1)} %q_ref.3) | copy-start | bytes 3145732
  0.7 51.0 %copy-start.1 = (bf16[128,4096]{1,0:T(8,128)(2,1)S(1)}, bf16[128,4096]{1,0:T(8,128)(2,1)}, u32[]{:S(2)}) copy-start(bf16[128,4096]{1,0:T(8,128)(2,1)} %g_ref.3) | copy-start | bytes 3145732
  0.7 25.6 %collective-permute-start.1 = (bf16[128,512]{1,0:T(8,128)(2,1)}, bf16[128,512]{1,0:T(8,128)(2,1)S(1)}, u32[]{:S(2)}, u32[]{:S(2)}) collective-permute-start(bf16[128,512]{1,0:T(8,128)(2,1)} %refs_0_.3), channel_id=1, source_target_pairs={{0,4},{1,3},{2,6},{3,5},{4,8},{5,7},{6,10},{7,9},{8,12},{9,11},{10... | collective-permute-start | bytes 393224 | tf_op jit(solution)/shard_map/ppermute | solution.py:23
  11.5 22.4 %collective-permute-start = (bf16[128,512]{1,0:T(8,128)(2,1)}, bf16[128,512]{1,0:T(8,128)(2,1)S(1)}, u32[]{:S(2)}, u32[]{:S(2)}) collective-permute-start(bf16[128,512]{1,0:T(8,128)(2,1)} %refs_0_.3), channel_id=1, source_target_pairs={{0,2},{1,5},{2,4},{3,7},{4,6},{5,9},{6,8},{7,11},{8,10},{9,13},{10... | collective-permute-start | bytes 393224 | tf_op jit(solution)/shard_map/ppermute | solution.py:23
  15.5 20.6 %collective-permute-start.4 = (bf16[128,512]{1,0:T(8,128)(2,1)}, bf16[128,512]{1,0:T(8,128)(2,1)S(1)}, u32[]{:S(2)}, u32[]{:S(2)}) collective-permute-start(bf16[128,512]{1,0:T(8,128)(2,1)} %refs_4_.1), channel_id=1, source_target_pairs={{0,4},{1,3},{2,6},{3,5},{4,8},{5,7},{6,10},{7,9},{8,12},{9,11},{10... | collective-permute-start | bytes 393224 | tf_op jit(solution)/shard_map/ppermute | solution.py:23
  17.9 23.8 %collective-permute-start.3 = (bf16[128,512]{1,0:T(8,128)(2,1)}, bf16[128,512]{1,0:T(8,128)(2,1)S(1)}, u32[]{:S(2)}, u32[]{:S(2)}) collective-permute-start(bf16[128,512]{1,0:T(8,128)(2,1)} %refs_4_.1), channel_id=1, source_target_pairs={{0,2},{1,5},{2,4},{3,7},{4,6},{5,9},{6,8},{7,11},{8,10},{9,13},{10... | collective-permute-start | bytes 393224 | tf_op jit(solution)/shard_map/ppermute | solution.py:23
  33.8 9.8 %collective-permute-start.2 = (bf16[256,512]{1,0:T(8,128)(2,1)S(1)}, bf16[256,512]{1,0:T(8,128)(2,1)S(1)}, u32[]{:S(2)}, u32[]{:S(2)}) collective-permute-start(bf16[256,512]{1,0:T(8,128)(2,1)S(1)} %pad_maximum_fusion), channel_id=1, source_target_pairs={{0,1},{1,0},{2,3},{3,2},{4,5},{5,4},{6,7},{7,6},{8,9},{9,8},{10,11... | collective-permute-start | bytes 786440 | tf_op jit(solution)/shard_map/ppermute | solution.py:30
  41.7 9.9 %collective-permute-start.5 = (bf16[256,512]{1,0:T(8,128)(2,1)S(1)}, bf16[256,512]{1,0:T(8,128)(2,1)S(1)}, u32[]{:S(2)}, u32[]{:S(2)}) collective-permute-start(bf16[256,512]{1,0:T(8,128)(2,1)S(1)} %pad_maximum_fusion.1), channel_id=1, source_target_pairs={{0,1},{1,0},{2,3},{3,2},{4,5},{5,4},{6,7},{7,6},{8,9},{9,8},{10,11... | collective-permute-start | bytes 786440 | tf_op jit(solution)/shard_map/ppermute | solution.py:30
  48.2 10.1 %collective-permute-start.9 = (bf16[256,512]{1,0:T(8,128)(2,1)S(1)}, bf16[256,512]{1,0:T(8,128)(2,1)S(1)}, u32[]{:S(2)}, u32[]{:S(2)}) collective-permute-start(bf16[256,512]{1,0:T(8,128)(2,1)S(1)} %get-tuple-element.20), channel_id=1, source_target_pairs={{0,1},{1,0},{2,3},{3,2},{4,5},{5,4},{6,7},{7,6},{8,9},{9,8},{10,11... | collective-permute-start | bytes 786440 | tf_op jit(solution)/shard_map/ppermute | solution.py:30
  56.4 18.4 %collective-permute-start.6 = (bf16[256,512]{1,0:T(8,128)(2,1)S(1)}, bf16[256,512]{1,0:T(8,128)(2,1)S(1)}, u32[]{:S(2)}, u32[]{:S(2)}) collective-permute-start(bf16[256,512]{1,0:T(8,128)(2,1)S(1)} %get-tuple-element.16), channel_id=1, source_target_pairs={{0,1},{1,0},{2,3},{3,2},{4,5},{5,4},{6,7},{7,6},{8,9},{9,8},{10,11... | collective-permute-start | bytes 786440 | tf_op jit(solution)/shard_map/ppermute | solution.py:30
  58.5 29.2 %collective-permute-start.10 = (bf16[128,512]{1,0:T(8,128)(2,1)S(1)}, bf16[128,512]{1,0:T(8,128)(2,1)S(1)}, u32[]{:S(2)}, u32[]{:S(2)}) collective-permute-start(bf16[128,512]{1,0:T(8,128)(2,1)S(1)} %get-tuple-element.23), channel_id=1, source_target_pairs={{0,510},{1,509},{2,0},{3,511},{4,2},{5,1},{6,4},{7,3},{8,6},{9,5},... | collective-permute-start | bytes 393224 | tf_op jit(solution)/shard_map/ppermute | solution.py:23
  72.9 14.8 %collective-permute-start.11 = (bf16[128,512]{1,0:T(8,128)(2,1)S(1)}, bf16[128,512]{1,0:T(8,128)(2,1)S(1)}, u32[]{:S(2)}, u32[]{:S(2)}) collective-permute-start(bf16[128,512]{1,0:T(8,128)(2,1)S(1)} %get-tuple-element.24), channel_id=1, source_target_pairs={{0,508},{1,511},{2,510},{3,1},{4,0},{5,3},{6,2},{7,5},{8,4},{9,7},... | collective-permute-start | bytes 393224 | tf_op jit(solution)/shard_map/ppermute | solution.py:23
  75.0 15.2 %collective-permute-start.7 = (bf16[128,512]{1,0:T(8,128)(2,1)S(1)}, bf16[128,512]{1,0:T(8,128)(2,1)S(1)}, u32[]{:S(2)}, u32[]{:S(2)}) collective-permute-start(bf16[128,512]{1,0:T(8,128)(2,1)S(1)} %get-tuple-element.25), channel_id=1, source_target_pairs={{0,510},{1,509},{2,0},{3,511},{4,2},{5,1},{6,4},{7,3},{8,6},{9,5},... | collective-permute-start | bytes 393224 | tf_op jit(solution)/shard_map/ppermute | solution.py:23
  85.8 10.3 %collective-permute-start.8 = (bf16[128,512]{1,0:T(8,128)(2,1)S(1)}, bf16[128,512]{1,0:T(8,128)(2,1)S(1)}, u32[]{:S(2)}, u32[]{:S(2)}) collective-permute-start(bf16[128,512]{1,0:T(8,128)(2,1)S(1)} %get-tuple-element.26), channel_id=1, source_target_pairs={{0,508},{1,511},{2,510},{3,1},{4,0},{5,3},{6,2},{7,5},{8,4},{9,7},... | collective-permute-start | bytes 393224 | tf_op jit(solution)/shard_map/ppermute | solution.py:23
